TPU v7x, 256 devices: a whole 4x4x8 slice. The times are simulated.
256 devices in a mesh: mp: 32 (over z, x), dp: 8 (over y, core).
Axes of the slice: x: 4, y: 4, z: 8, core: 2. Of those that a mesh axis runs over, the one named last changes fastest.
Arguments:
- inputs: bfloat16 [1536, 8192], P('dp', 'mp'), may hold values from -42 to 42
- out_grads: bfloat16 [1536, 16384], P('dp', 'mp'), may hold values from -42 to 42
- weight: bfloat16 [8192, 16384], P('dp', 'mp'), may hold values from -0.25 to 0.25
- enc_in: bfloat16 [8192, 1920], P('mp'), may hold values from -0.0625 to 0.0625
- dec_in: bfloat16 [1920, 8192], P(None, 'mp'), may hold values from -0.125 to 0.125
- enc_out: bfloat16 [16384, 1920], P('mp'), may hold values from -0.046875 to 0.046875
- dec_out: bfloat16 [1920, 16384], P(None, 'mp'), may hold values from -0.125 to 0.125
Outputs:
- post_out: bfloat16 [1536, 16384], P('dp', 'mp')
- grad_in: bfloat16 [1536, 8192], P('dp', 'mp')
All inputs are finite; a program needn't handle non-finite values.
Results may differ from a plain program's by a relative error of at most 0.024.
Values may be sent and summed in bfloat16 or wider, within the bound.
A program may use at most 64 MiB of HBM per device.

v0:
```python
import jax
import jax.numpy as jnp
from jax import lax
from jax.sharding import PartitionSpec as P

D = 8192
FW = 16384


epsilon = 1e-06
step_size = 0.25


def silu_slope(value):
    sig = jax.nn.sigmoid(value)
    return sig * (1.0 + value * (1.0 - sig))


def shards(inputs, out_grads, weight, enc_in, dec_in, enc_out, dec_out):
    factor = step_size / D
    input_wide = inputs.astype(jnp.float32)
    grad_wide = out_grads.astype(jnp.float32)
    input_sq = jnp.sum(input_wide * input_wide, axis=1)
    grad_sq = jnp.sum(grad_wide * grad_wide, axis=1)
    input_proj = jnp.dot(inputs, enc_in, preferred_element_type=jnp.float32)
    grad_proj = jnp.dot(out_grads, enc_out, preferred_element_type=jnp.float32)
    input_total, grad_total = lax.psum((input_sq, grad_sq), "mp")
    input_proj, grad_proj = (
        lax.psum(input_proj.astype(jnp.bfloat16), "mp").astype(jnp.float32),
        lax.psum(grad_proj.astype(jnp.bfloat16), "mp").astype(jnp.float32),
    )
    input_scale = lax.rsqrt(input_total / D + epsilon)[:, None]
    grad_scale = lax.rsqrt(grad_total / FW + epsilon)[:, None]
    input_hidden = jax.nn.relu(input_proj * input_scale).astype(jnp.bfloat16)
    grad_hidden = jax.nn.relu(grad_proj * grad_scale).astype(jnp.bfloat16)
    edited_in = (
        input_wide + jnp.dot(input_hidden, dec_in, preferred_element_type=jnp.float32)
    ).astype(jnp.bfloat16)
    edited_grad = (
        grad_wide + jnp.dot(grad_hidden, dec_out, preferred_element_type=jnp.float32)
    ).astype(jnp.bfloat16)
    whole_in = lax.all_gather(inputs, "mp", axis=1, tiled=True)
    edits_all = lax.all_gather(edited_in, "dp", axis=0, tiled=True)
    grads_all = lax.all_gather(edited_grad, "dp", axis=0, tiled=True)
    kernel = lax.psum(
        jnp.dot(inputs, edits_all.T, preferred_element_type=jnp.float32).astype(jnp.bfloat16), "mp"
    ).astype(jnp.float32)
    kernel = (kernel * factor).astype(jnp.bfloat16)
    base_out = jnp.dot(
        whole_in,
        lax.all_gather(weight, "dp", axis=0, tiled=True),
        preferred_element_type=jnp.float32,
    )
    post_full = base_out - jnp.dot(kernel, grads_all, preferred_element_type=jnp.float32)
    cotangent = (grad_wide * silu_slope(post_full)).astype(jnp.bfloat16)
    back_kernel = lax.psum(
        jnp.dot(cotangent, grads_all.T, preferred_element_type=jnp.float32).astype(jnp.bfloat16),
        "mp",
    ).astype(jnp.float32)
    back_kernel = (back_kernel * factor).astype(jnp.bfloat16)
    partial_value = jnp.dot(
        cotangent,
        lax.all_gather(weight, "dp", axis=0, tiled=True).T,
        preferred_element_type=jnp.float32,
    )
    back_sum = lax.psum_scatter(
        partial_value.astype(jnp.bfloat16), "mp", scatter_dimension=1, tiled=True
    ).astype(jnp.float32)
    grad_in = (
        back_sum - jnp.dot(back_kernel, edits_all, preferred_element_type=jnp.float32)
    ).astype(jnp.bfloat16)
    return (post_full.astype(jnp.bfloat16), grad_in)


def solution(mesh):
    in_specs = (
        P("dp", "mp"),
        P("dp", "mp"),
        P("dp", "mp"),
        P("mp", None),
        P(None, "mp"),
        P("mp", None),
        P(None, "mp"),
    )
    out_specs = (P("dp", "mp"), P("dp", "mp"))
    return jax.shard_map(shards, mesh=mesh, in_specs=in_specs, out_specs=out_specs, check_vma=False)
```

profile of v0, /device:TPU:8, one launch (start us, length us, event | category | flops | bytes accessed | tf_op | source)
XLA Modules:
  0.0 874.0 jit_solution(16068317335428372301)
XLA Ops:
  7.2 0.0 copy-start
  7.2 0.0 copy-start.1
  7.2 0.0 copy-start.4
  7.2 0.0 all-reduce.6.cloned.1.call-start
  7.2 2.7 convolution_convert_fusion.4
  9.9 0.0 all-reduce.6.cloned.1.call-update
  9.9 0.0 all-reduce.10.cloned.1.call-start
  10.0 0.0 copy-done.1
  10.0 0.1 fusion.12
  10.1 0.0 copy-done.4
  10.1 0.1 fusion.10
  10.2 77.8 %all-reduce = (f32[192]{0:T(256)S(1)}, f32[192]{0:T(256)S(1)}) all-reduce(f32[192]{0:T(256)S(1)} %fusion.10, f32[192]{0:T(256)S(1)} %fusion.12), channel_id=1, replica_groups=mesh['mp'=32,'dp'=8] {'mp'}, use_global_device_ids=true, to_apply=%region_6.7 | all-reduce | flops 384 | bytes 3072 | tf_op jit(solution)/shard_map/psum | solution.py:27
  88.0 0.0 copy-done
  88.0 1.5 convolution_convert_fusion.3
  89.5 73.4 %all-reduce.6.cloned.1.call-done = bf16[192,1920]{1,0:T(8,128)(2,1)} async-done(((bf16[192,1920]{1,0:T(8,128)(2,1)}), bf16[192,1920]{1,0:T(8,128)(2,1)}) %all-reduce.6.cloned.1.call-update) | async-done | bytes 737296 | tf_op jit(solution)/shard_map/psum | solution.py:29
  162.9 1.9 fusion.2
  164.8 13.5 %all_gather.15 = bf16[1536,256]{1,0:T(8,128)(2,1)S(1)} all-gather(bf16[192,256]{1,0:T(8,128)(2,1)S(1)} %fusion.2), channel_id=1, replica_groups=mesh['mp'=32,'dp'=8] {'dp'}, dimensions={0}, use_global_device_ids=true | all-gather | bytes 884736 | tf_op jit(solution)/shard_map/all_gather | solution.py:43
  178.3 1.3 fusion
  179.6 0.0 all-reduce.10.cloned.1.call-update
  179.6 0.0 all-gather.4.cloned.1.call-start
  179.7 0.7 all-gather.4.cloned.1.call-update
  180.4 0.0 all-gather.6.cloned.1.call-start
  180.4 0.5 all-gather.6.cloned.1.call-update
  180.9 0.0 all-gather.8.cloned.1.call-start
  181.0 147.2 %all-reduce.10.cloned.1.call-done = (bf16[192,1920]{1,0:T(8,128)(2,1)}, bf16[192,1536]{0,1:T(8,128)(2,1)}) async-done(((bf16[192,1920]{1,0:T(8,128)(2,1)}, bf16[192,1536]{0,1:T(8,128)(2,1)}), (bf16[192,1920]{1,0:T(8,128)(2,1)}, bf16[192,1536]{0,1:T(8,128)(2,1)})) %all-reduce.10.cloned.1.call-update) | async-done | bytes 1327120 | tf_op jit(solution)/shard_map/psum | solution.py:30
  328.2 3.1 fusion.1
  331.3 0.0 all-gather.8.cloned.1.call-update
  331.3 0.0 copy-start.3
  331.3 0.0 all-reduce.8.cloned.1.call-start
  331.4 75.0 %all-gather.4.cloned.1.call-done = bf16[192,8192]{1,0:T(8,128)(2,1)} async-done(((bf16[192,256]{1,0:T(8,128)(2,1)}), bf16[192,8192]{1,0:T(8,128)(2,1)}) %all-gather.4.cloned.1.call-update) | async-done | bytes 3145744 | tf_op jit(solution)/shard_map/all_gather | solution.py:42
  406.4 53.9 %all-gather.6.cloned.1.call-done = bf16[8192,512]{1,0:T(8,128)(2,1)} async-done(((bf16[1024,512]{1,0:T(8,128)(2,1)}), bf16[8192,512]{1,0:T(8,128)(2,1)}) %all-gather.6.cloned.1.call-update) | async-done | bytes 8388624 | tf_op jit(solution)/shard_map/all_gather | solution.py:51
  460.3 6.9 fusion.20
  467.2 22.0 %all-gather.8.cloned.1.call-done = bf16[1536,512]{1,0:T(8,128)(2,1)} async-done(((bf16[192,512]{1,0:T(8,128)(2,1)}), bf16[1536,512]{1,0:T(8,128)(2,1)}) %all-gather.8.cloned.1.call-update) | async-done | bytes 1572880 | tf_op jit(solution)/shard_map/all_gather | solution.py:44
  489.2 0.0 copy-done.3
  489.2 0.0 copy-start.2
  489.2 0.0 copy-start.5
  489.2 2.9 fusion.19
  492.1 0.0 copy-done.2
  492.1 0.0 copy-done.5
  492.1 2.6 convolution_convert_fusion.2
  494.8 0.0 all-reduce.8.cloned.1.call-update
  494.8 0.0 reduce-scatter.2.cloned.1.call-start
  494.8 0.0 copy-done.6
  494.9 8.1 convolution_convert_fusion
  502.9 0.0 reduce-scatter.2.cloned.1.call-update
  503.0 142.1 %all-reduce.8.cloned.1.call-done = bf16[192,1536]{0,1:T(8,128)(2,1)} async-done(((bf16[192,1536]{0,1:T(8,128)(2,1)}), bf16[192,1536]{0,1:T(8,128)(2,1)}) %all-reduce.8.cloned.1.call-update) | async-done | bytes 589840 | tf_op jit(solution)/shard_map/psum | solution.py:56
  645.1 219.9 %reduce-scatter.2.cloned.1.call-done = bf16[192,256]{1,0:T(8,128)(2,1)} async-done(((bf16[192,8192]{1,0:T(8,128)(2,1)}), bf16[192,256]{1,0:T(8,128)(2,1)}) %reduce-scatter.2.cloned.1.call-update) | async-done | bytes 98320 | tf_op jit(solution)/shard_map/reduce_scatter | solution.py:66
  865.0 2.2 fusion.3
  (3 shorter events, 0.0 us)
Async XLA Ops:
  7.2 80.9 %copy-start = (bf16[512,1920]{1,0:T(8,128)(2,1)S(1)}, bf16[512,1920]{1,0:T(8,128)(2,1)}, u32[]{:S(2)}) copy-start(bf16[512,1920]{1,0:T(8,128)(2,1)} %param.12) | copy-start | bytes 5898244
  7.2 2.8 copy-start.1
  7.2 2.9 copy-start.4
  7.2 155.7 %all-reduce.6.cloned.1.call-start = ((), (), s32[]{:S(2)}) async-start(), calls=%async_computation.3 | async-start | bytes 1474560 | tf_op jit(solution)/shard_map/psum | solution.py:29
  9.9 318.3 %all-reduce.10.cloned.1.call-start = ((), (), s32[]{:S(2)}) async-start(), calls=%async_computation.7 | async-start | bytes 3047424 | tf_op jit(solution)/shard_map/psum | solution.py:30
  179.6 226.8 %all-gather.4.cloned.1.call-start = ((), (), s32[]{:S(2)}) async-start(), calls=%async_computation.1 | async-start | bytes 3244032 | tf_op jit(solution)/shard_map/all_gather | solution.py:42
  180.4 280.0 %all-gather.6.cloned.1.call-start = ((), (), s32[]{:S(2)}) async-start(), calls=%async_computation.2 | async-start | bytes 9437184 | tf_op jit(solution)/shard_map/all_gather | solution.py:51
  180.9 308.3 %all-gather.8.cloned.1.call-start = ((), (), s32[]{:S(2)}) async-start(), calls=%async_computation.4 | async-start | bytes 1769472 | tf_op jit(solution)/shard_map/all_gather | solution.py:44
  331.3 157.9 %copy-start.3 = (bf16[192,1536]{0,1:T(8,128)(2,1)S(1)}, bf16[192,1536]{0,1:T(8,128)(2,1)}, u32[]{:S(2)}) copy-start(bf16[192,1536]{0,1:T(8,128)(2,1)} %get-tuple-element.5) | copy-start | bytes 1769476
  331.3 313.8 %all-reduce.8.cloned.1.call-start = ((), (), s32[]{:S(2)}) async-start(), calls=%async_computation.6 | async-start | bytes 1572864 | tf_op jit(solution)/shard_map/psum | solution.py:56
  489.2 2.9 copy-start.2
  489.2 2.9 copy-start.5
  492.1 2.7 copy-start.6
  494.8 370.2 %reduce-scatter.2.cloned.1.call-start = ((), (), s32[]{:S(2)}) async-start(), calls=%async_computation.5 | async-start | bytes 3244032 | tf_op jit(solution)/shard_map/reduce_scatter | solution.py:66
Sparse Core Ops, SparseCore 0:
  11.4 151.4 all-reduce.5
  179.7 148.4 all-reduce.9
  331.0 75.3 all-gather.3
  408.3 51.9 all-gather.5
  462.7 26.4 all-gather.7
  494.9 150.1 all-reduce.7
  649.5 215.4 reduce-scatter.1
where the time goes:
time: 874 us
  waiting for transfers between devices  735 us (84%)
  blocking collectives  91.3 us (10%)
  matrix products  33.1 us (4%)
  between operations  14.2 us (2%)
    reduce_scatter x1, waiting for transfers between devices, shards(): lax.psum_scatter(partial_value.astype(jnp.bfloat16), 'mp', scatter_dimens...  220 us
    psum x1, waiting for transfers between devices, shards(): lax.psum(grad_proj.astype(jnp.bfloat16), 'mp').astype(jnp.float32)  147 us
    psum x1, waiting for transfers between devices, shards(): lax.psum(jnp.dot(cotangent, grads_all.T, preferred_element_type=jnp.float...  142 us
    psum x1, blocking collectives, shards(): input_total, grad_total = lax.psum((input_sq, grad_sq), 'mp')  77.8 us
    all_gather x1, waiting for transfers between devices, shards(): whole_in = lax.all_gather(inputs, 'mp', axis=1, tiled=True)  75 us
    psum x1, waiting for transfers between devices, shards(): lax.psum(input_proj.astype(jnp.bfloat16), 'mp').astype(jnp.float32)  73.4 us
    all_gather x1, waiting for transfers between devices, shards(): lax.all_gather(weight, 'dp', axis=0, tiled=True)  53.9 us
    all_gather x1, waiting for transfers between devices, shards(): grads_all = lax.all_gather(edited_grad, 'dp', axis=0, tiled=True)  22 us
  transfers between devices with their start and end apart: 7, of which 7 were waited for; matrix products, arithmetic and copies ran while one was open for 2% of the time, Pallas kernels for 0%

commit v1 on v0

v1 whole, which is shorter than its diff:
```python
import functools

import jax
import jax.numpy as jnp
from jax import lax
from jax.experimental import pallas as pl
from jax.experimental.pallas import tpu as pltpu
from jax.sharding import PartitionSpec as P

D = 8192
FW = 16384
R = 1920
NZ, NX, NY = 8, 4, 4
TOK = 192
ROWS = TOK // NX
epsilon = 1e-06
FACTOR = 0.25 / D
F32 = jnp.float32
BF16 = jnp.bfloat16
MESH = pl.DeviceIdType.MESH


def nn(a, b):
    return lax.dot_general(a, b, (((1,), (0,)), ((), ())), preferred_element_type=F32)


def nt(a, b):
    return lax.dot_general(a, b, (((1,), (1,)), ((), ())), preferred_element_type=F32)


class Links:
    def __init__(self, send, recv):
        self.send, self.recv, self.used, self.sent = send, recv, 0, []
        mp, dp = lax.axis_index("mp"), lax.axis_index("dp")
        self.z, self.x = mp // NX, mp % NX
        self.y, self.c = dp // 2, dp % 2

    def at(self, z=None, x=None, y=None, c=None):
        z = self.z if z is None else z
        x = self.x if x is None else x
        y = self.y if y is None else y
        c = self.c if c is None else c
        return (z * NX + x, y * 2 + c)

    def copy(self, src, dst, device):
        k = self.used
        self.used += 1
        made = pltpu.make_async_remote_copy(
            src_ref=src, dst_ref=dst, send_sem=self.send.at[k], recv_sem=self.recv.at[k],
            device_id=device, device_id_type=MESH)
        made.start()
        self.sent.append(made)
        return made


class AllReduce:
    def __init__(self, net, part, got_x, row, got_z, full):
        self.net, self.part, self.got_x, self.row, self.got_z, self.full = net, part, got_x, row, got_z, full

    def scatter_x(self):
        n = self.net
        self.a = [n.copy(self.part.at[(n.x + o) % NX], self.got_x.at[o - 1], n.at(x=(n.x + o) % NX))
                  for o in range(1, NX)]

    def scatter_z(self):
        n = self.net
        for made in self.a:
            made.wait_recv()

        def add(k, _):
            total = self.part[n.x, k].astype(F32)
            for o in range(NX - 1):
                total = total + self.got_x[o, k].astype(F32)
            self.row[k] = total.astype(BF16)
            return 0
        lax.fori_loop(0, NZ, add, 0)
        self.b = [n.copy(self.row.at[(n.z + o) % NZ], self.got_z.at[o - 1], n.at(z=(n.z + o) % NZ))
                  for o in range(1, NZ)]

    def gather_z(self):
        n = self.net
        for made in self.b:
            made.wait_recv()
        total = self.row[n.z].astype(F32)
        for o in range(NZ - 1):
            total = total + self.got_z[o].astype(F32)
        self.full[n.x, n.z] = total.astype(BF16)
        self.d = [n.copy(self.full.at[n.x, n.z], self.full.at[n.x, n.z], n.at(z=(n.z + o) % NZ))
                  for o in range(1, NZ)]

    def gather_x(self):
        n = self.net
        for made in self.d:
            made.wait_recv()
        self.e = [n.copy(self.full.at[n.x], self.full.at[n.x], n.at(x=(n.x + o) % NX))
                  for o in range(1, NX)]

    def done(self):
        for made in self.e:
            made.wait_recv()


class GatherDp:
    def __init__(self, net, part):
        self.net, self.part = net, part

    def start(self, src=None):
        n = self.net
        d = n.y * 2 + n.c
        own = self.part(d, None)
        src = own if src is None else src
        self.up = n.copy(src, own, n.at(y=(n.y + 1) % NY))
        self.down = n.copy(src, own, n.at(y=(n.y + NY - 1) % NY))
        self.over = [n.copy(src, own, n.at(c=1 - n.c))]

    def relay(self):
        n = self.net
        below = ((n.y + NY - 1) % NY) * 2 + n.c
        above = ((n.y + 1) % NY) * 2 + n.c
        self.up.wait_recv()
        self.up2 = n.copy(self.part(below, 0), self.part(below, 0), n.at(y=(n.y + 1) % NY))
        self.over.append(n.copy(self.part(below, None), self.part(below, None), n.at(c=1 - n.c)))
        self.down.wait_recv()
        self.down2 = n.copy(self.part(above, 1), self.part(above, 1), n.at(y=(n.y + NY - 1) % NY))
        self.over.append(n.copy(self.part(above, None), self.part(above, None), n.at(c=1 - n.c)))

    def relay_far(self):
        n = self.net
        far = ((n.y + 2) % NY) * 2 + n.c
        self.up2.wait_recv()
        self.over.append(n.copy(self.part(far, 0), self.part(far, 0), n.at(c=1 - n.c)))
        self.down2.wait_recv()
        self.over.append(n.copy(self.part(far, 1), self.part(far, 1), n.at(c=1 - n.c)))

    def done(self):
        for made in self.over:
            made.wait_recv()


class GatherMp:
    def __init__(self, net, block):
        self.net, self.block = net, block

    def start(self):
        n = self.net
        own = self.block.at[n.z, n.x]
        self.a = [n.copy(own, own, n.at(x=(n.x + o) % NX)) for o in range(1, NX)]
        self.s = 0

    def step(self):
        n, s = self.net, self.s
        if s == 0:
            for made in self.a:
                made.wait_recv()
        else:
            self.up.wait_recv()
            if s <= NZ // 2 - 1:
                self.down.wait_recv()
        if s < NZ // 2:
            up = self.block.at[(n.z + NZ - s) % NZ]
            self.up = n.copy(up, up, n.at(z=(n.z + 1) % NZ))
        if s < NZ // 2 - 1:
            down = self.block.at[(n.z + s) % NZ]
            self.down = n.copy(down, down, n.at(z=(n.z + NZ - 1) % NZ))
        self.s += 1


def body(x_hbm, g_hbm, w_hbm, ei_hbm, di_hbm, eo_hbm, do_hbm, post_ref, gin_ref,
         xin, g, w, ei, di, eo, do, part, got_x, row, got_z, full, edits, grads, total, cot,
         bpart, bgot_x, brow, bgot_z, send, recv, load):
    net = Links(send, recv)
    z, x, y, c = net.z, net.x, net.y, net.c
    d = y * 2 + c

    loads = []
    for k, (src, dst) in enumerate(((x_hbm, xin.at[z, x]), (ei_hbm, ei), (g_hbm, g), (eo_hbm, eo),
                                    (di_hbm, di), (do_hbm, do), (w_hbm, w.at[d]))):
        made = pltpu.make_async_copy(src, dst, load.at[k])
        made.start()
        loads.append(made)

    barrier = pltpu.get_barrier_semaphore()
    peers = ([net.at(x=(x + o) % NX) for o in range(1, NX)] + [net.at(z=(z + o) % NZ) for o in range(1, NZ)]
             + [net.at(y=(y + 1) % NY), net.at(y=(y + NY - 1) % NY), net.at(c=1 - c)])
    for peer in peers:
        pl.semaphore_signal(barrier, inc=1, device_id=peer, device_id_type=MESH)
    pl.semaphore_wait(barrier, len(peers))

    def w_part(slot, half):
        return w.at[slot] if half is None else w.at[slot, pl.ds(2 * half, 2)]

    def rows_of(ref):
        def pick(slot, half):
            return ref.at[slot, pl.ds(0, TOK)] if half is None else ref.at[slot, pl.ds(half * (TOK // 2), TOK // 2)]
        return pick

    whole_w = GatherDp(net, w_part)
    whole_w.start(w_hbm)
    loads[0].wait()
    whole_in = GatherMp(net, xin)
    whole_in.start()

    own = xin[z, x]

    def project(value, enc, out):
        for k in range(7):
            block = nn(value, enc[:, 256 * k:256 * k + 256])
            out[:, k] = block.astype(BF16).reshape(NX, ROWS, 256)
        last = nn(value, enc[:, 1792:1920])
        out[:, 7, :, 0:128] = last.astype(BF16).reshape(NX, ROWS, 128)
        wide = value.astype(F32)
        square = wide * wide
        fold = square[:, 0:128]
        for k in range(1, value.shape[1] // 128):
            fold = fold + square[:, 128 * k:128 * k + 128]
        out[:, 7, :, 128:256] = fold.astype(BF16).reshape(NX, ROWS, 128)

    reduce_in, reduce_out, reduce_kernel, reduce_back = [
        AllReduce(net, part.at[k], got_x.at[k], row.at[k], got_z.at[k], full.at[k]) for k in range(4)]

    loads[1].wait()
    project(own, ei, part.at[0])
    reduce_in.scatter_x()
    loads[2].wait()
    loads[3].wait()
    project(g[...], eo, part.at[1])
    reduce_out.scatter_x()
    edits[:, pl.ds(TOK, 256 - TOK)] = jnp.zeros((8, 256 - TOK, 256), BF16)
    grads[:, pl.ds(TOK, 256 - TOK)] = jnp.zeros((8, 256 - TOK, 512), BF16)
    for made in loads[4:]:
        made.wait()
    whole_in.step()
    reduce_in.scatter_z()
    reduce_out.scatter_z()
    reduce_in.gather_z()
    reduce_out.gather_z()
    whole_in.step()
    reduce_in.gather_x()
    reduce_out.gather_x()
    whole_w.relay()

    def edit(value, hidden, dec, features):
        squares = hidden[:, 7, :, 128:256].astype(F32).reshape(TOK, 128)
        scale = lax.rsqrt(jnp.sum(squares, axis=1, keepdims=True) / features + epsilon)
        out = value.astype(F32)
        for k in range(8):
            width = 256 if k < 7 else 128
            h = hidden[:, k, :, 0:width].astype(F32).reshape(TOK, width)
            h = jnp.maximum(h * scale, 0.0).astype(BF16)
            out = out + nn(h, dec[256 * k:256 * k + width, :])
        return out.astype(BF16)

    gather_edits = GatherDp(net, rows_of(edits))
    gather_grads = GatherDp(net, rows_of(grads))
    reduce_in.done()
    edits[d, pl.ds(0, TOK)] = edit(own, full.at[0], di, D)
    gather_edits.start()
    reduce_out.done()
    grads[d, pl.ds(0, TOK)] = edit(g[...], full.at[1], do, FW)
    gather_grads.start()
    gather_edits.relay()
    gather_edits.relay_far()
    gather_edits.done()

    def inner(k, _):
        part[2, :, k] = nt(own, edits[k]).astype(BF16).reshape(NX, ROWS, 256)
        return 0
    lax.fori_loop(0, 8, inner, 0)
    reduce_kernel.scatter_x()
    gather_grads.relay()
    whole_in.step()
    whole_w.relay_far()
    reduce_kernel.scatter_z()
    gather_grads.relay_far()
    whole_in.step()
    reduce_kernel.gather_z()
    whole_w.done()
    whole_in.step()

    total[...] = jnp.zeros_like(total)

    def base(k, _):
        value = nn(xin[k, 0], w[k, 0])
        for j in range(1, NX):
            value = value + nn(xin[k, j], w[k, j])
        total[...] += value
        return 0
    lax.fori_loop(0, NZ, base, 0)
    reduce_kernel.gather_x()
    gather_grads.done()
    reduce_kernel.done()

    def correct(k, _):
        block = (full[2, :, k].astype(F32) * FACTOR).astype(BF16).reshape(TOK, 256)
        total[...] -= nn(block, grads[k])
        return 0
    lax.fori_loop(0, 8, correct, 0)

    def activate(k, _):
        rows = pl.ds(k * ROWS, ROWS)
        post = total[rows, :]
        post_ref[rows, :] = post.astype(BF16)
        sig = jax.nn.sigmoid(post)
        cot[rows, :] = (g[rows, :].astype(F32) * (sig * (1.0 + post * (1.0 - sig)))).astype(BF16)
        return 0
    lax.fori_loop(0, NX, activate, 0)

    def back_inner(k, _):
        part[3, :, k] = nt(cot[...], grads[k]).astype(BF16).reshape(NX, ROWS, 256)
        return 0
    lax.fori_loop(0, 8, back_inner, 0)
    reduce_back.scatter_x()

    def back_for(j):
        def one(k, _):
            bpart[j, k] = nt(cot[...], w[k, j]).astype(BF16)
            return 0
        lax.fori_loop(0, NZ, one, 0)

    first = []
    for o in range(1, NX):
        j = (x + o) % NX
        back_for(j)
        first.append(net.copy(bpart.at[j], bgot_x.at[o - 1], net.at(x=j)))
    back_for(x)
    reduce_back.scatter_z()
    reduce_back.gather_z()
    reduce_back.gather_x()
    for made in first:
        made.wait_recv()

    def back_add(k, _):
        value = bpart[x, k].astype(F32)
        for o in range(NX - 1):
            value = value + bgot_x[o, k].astype(F32)
        brow[k] = value.astype(BF16)
        return 0
    lax.fori_loop(0, NZ, back_add, 0)
    second = [net.copy(brow.at[(z + o) % NZ], bgot_z.at[o - 1], net.at(z=(z + o) % NZ)) for o in range(1, NZ)]
    reduce_back.done()
    result = jnp.zeros((TOK, 256), F32)
    for k in range(8):
        block = (full[3, :, k].astype(F32) * FACTOR).astype(BF16).reshape(TOK, 256)
        result = result - nn(block, edits[k])
    result = result + brow[z].astype(F32)
    for o, made in enumerate(second):
        made.wait_recv()
        result = result + bgot_z[o].astype(F32)
    gin_ref[...] = result.astype(BF16)

    for made in net.sent:
        made.wait_send()


COPIES = 160


def shards(inputs, out_grads, weight, enc_in, dec_in, enc_out, dec_out):
    anywhere = pl.BlockSpec(memory_space=pl.ANY)
    vmem = pl.BlockSpec(memory_space=pltpu.VMEM)
    scratch = [
        pltpu.VMEM((NZ, NX, TOK, 256), BF16),
        pltpu.VMEM((TOK, 512), BF16),
        pltpu.VMEM((8, 4, 256, 512), BF16),
        pltpu.VMEM((256, R), BF16),
        pltpu.VMEM((R, 256), BF16),
        pltpu.VMEM((512, R), BF16),
        pltpu.VMEM((R, 512), BF16),
        pltpu.VMEM((4, NX, NZ, ROWS, 256), BF16),
        pltpu.VMEM((4, NX - 1, NZ, ROWS, 256), BF16),
        pltpu.VMEM((4, NZ, ROWS, 256), BF16),
        pltpu.VMEM((4, NZ - 1, ROWS, 256), BF16),
        pltpu.VMEM((4, NX, NZ, ROWS, 256), BF16),
        pltpu.VMEM((8, 256, 256), BF16),
        pltpu.VMEM((8, 256, 512), BF16),
        pltpu.VMEM((TOK, 512), F32),
        pltpu.VMEM((TOK, 512), BF16),
        pltpu.VMEM((NX, NZ, TOK, 256), BF16),
        pltpu.VMEM((NX - 1, NZ, TOK, 256), BF16),
        pltpu.VMEM((NZ, TOK, 256), BF16),
        pltpu.VMEM((NZ - 1, TOK, 256), BF16),
        pltpu.SemaphoreType.DMA((COPIES,)),
        pltpu.SemaphoreType.DMA((COPIES,)),
        pltpu.SemaphoreType.DMA((7,)),
    ]
    return pl.pallas_call(
        body,
        out_shape=(jax.ShapeDtypeStruct((TOK, 512), BF16), jax.ShapeDtypeStruct((TOK, 256), BF16)),
        in_specs=[anywhere] * 7,
        out_specs=(vmem, vmem),
        scratch_shapes=scratch,
        compiler_params=pltpu.CompilerParams(
            collective_id=0, has_side_effects=True, vmem_limit_bytes=60 * 1024 * 1024),
    )(inputs, out_grads, weight.reshape(4, 256, 512), enc_in, dec_in, enc_out, dec_out)


def solution(mesh):
    in_specs = (
        P("dp", "mp"),
        P("dp", "mp"),
        P("dp", "mp"),
        P("mp", None),
        P(None, "mp"),
        P("mp", None),
        P(None, "mp"),
    )
    out_specs = (P("dp", "mp"), P("dp", "mp"))
    return jax.shard_map(shards, mesh=mesh, in_specs=in_specs, out_specs=out_specs, check_vma=False)
```

time: 874 us -> 189 us (0.22)
  waiting for transfers between devices: 735 us -> 0 us
  Pallas kernels: 0 us -> 182 us
  blocking collectives: 91.3 us -> 0 us
  matrix products: 33.1 us -> 0 us
  between operations: 14.2 us -> 0.64 us
    psum x3 -> x0, waiting for transfers between devices: 363 us -> none  [the longest x1 147 us: shards(): lax.psum(grad_proj.astype(jnp.bfloat16), 'mp').astype(jnp.float32)]
    reduce_scatter x1 -> x0, waiting for transfers between devices: 220 us -> none  [shards(): lax.psum_scatter(partial_value.astype(jnp.bfloat16), 'mp', scatter_dimens...]
    pallas_call x0 -> x1, Pallas kernels: none -> 182 us  [shards(): pl.pallas_call(body, out_shape=(jax.ShapeDtypeStruct((TOK, 512), BF16), j...]
    all_gather x3 -> x0, waiting for transfers between devices: 151 us -> none  [the longest x1 75 us: shards(): whole_in = lax.all_gather(inputs, 'mp', axis=1, tiled=True)]
    psum x1 -> x0, blocking collectives: 77.8 us -> none  [shards(): input_total, grad_total = lax.psum((input_sq, grad_sq), 'mp')]
    dot_general x10 -> x0, matrix products: 33.1 us -> none  [the longest x1 8.09 us: shards(): jnp.dot(cotangent, lax.all_gather(weight, 'dp', axis=0, tiled=True).T, pr...]
    all_gather x1 -> x0, blocking collectives: 13.5 us -> none  [shards(): edits_all = lax.all_gather(edited_in, 'dp', axis=0, tiled=True)]
  transfers between devices with their start and end apart: 7 -> 0, of which waited for: 7 -> 0; matrix products, arithmetic and copies ran while one was open for 2% -> 0% of each run, Pallas kernels for 0% -> 0%
where the time goes in v1:
time: 189 us; the launch traced here: 186 us
  Pallas kernels  182 us (96%)
  local copies, waits for them, and re-layouts  3.16 us (2%)
    pallas_call x1, Pallas kernels, shards(): pl.pallas_call(body, out_shape=(jax.ShapeDtypeStruct((TOK, 512), BF16), j...  182 us

profile of v1, /device:TPU:8, one launch (start us, length us, event | category | flops | bytes accessed | tf_op | source)
XLA Modules:
  0.0 185.7 jit_solution(2434461535541672797)
XLA Ops:
  0.6 181.9 %shard_map.86 = (bf16[192,512]{1,0:T(8,128)(2,1)}, bf16[192,256]{1,0:T(8,128)(2,1)}) custom-call(bf16[192,256]{1,0:T(8,128)(2,1)} %x_hbm.1, bf16[192,512]{1,0:T(8,128)(2,1)} %g_hbm.1, bf16[4,256,512]{2,1,0:T(8,128)(2,1)} %bitcast.1, bf16[256,1920]{1,0:T(8,128)(2,1)} %ei_hbm.1, bf16[1920,256]{1,0:T(8,128)(2,1)} %di_hbm.1, bf16[512,1920]{1,0:T(8,128)(2,1)} %eo_hbm.1, ...), custom_call_target="tpu_custom_call" | custom-call | tf_op jit(solution)/shard_map/pallas_call | solution.py:386
  182.5 1.6 copy.11
  184.1 1.5 copy.12

commit v2 on v1

--- a/solution.py
+++ b/solution.py
@@ -28,6 +28,13 @@
     return lax.dot_general(a, b, (((1,), (1,)), ((), ())), preferred_element_type=F32)
 
 
+def given(when, act):
+    if when is None:
+        act()
+    else:
+        pl.when(when)(act)
+
+
 class Links:
     def __init__(self, send, recv):
         self.send, self.recv, self.used, self.sent = send, recv, 0, []
@@ -42,24 +49,38 @@
         c = self.c if c is None else c
         return (z * NX + x, y * 2 + c)
 
-    def copy(self, src, dst, device):
+    def copy(self, src, dst, device, when=None):
         k = self.used
         self.used += 1
         made = pltpu.make_async_remote_copy(
             src_ref=src, dst_ref=dst, send_sem=self.send.at[k], recv_sem=self.recv.at[k],
             device_id=device, device_id_type=MESH)
-        made.start()
-        self.sent.append(made)
+        given(when, made.start)
+        self.sent.append((made, when))
         return made
 
+    def finish(self):
+        for made, when in self.sent:
+            given(when, made.wait_send)
+
 
 class AllReduce:
-    def __init__(self, net, part, got_x, row, got_z, full):
+    def __init__(self, net, part, got_x, row, got_z, full, blocks=NZ):
         self.net, self.part, self.got_x, self.row, self.got_z, self.full = net, part, got_x, row, got_z, full
+        self.blocks = blocks
+
+    def all(self, ref, i):
+        return ref.at[i] if self.blocks == NZ else ref.at[i, pl.ds(0, self.blocks)]
+
+    def keeps(self, z):
+        return None if self.blocks == NZ else z % 4 != 3
+
+    def block(self, z):
+        return z if self.blocks == NZ else z // 4 * 3 + jnp.minimum(z % 4, 2)
 
     def scatter_x(self):
         n = self.net
-        self.a = [n.copy(self.part.at[(n.x + o) % NX], self.got_x.at[o - 1], n.at(x=(n.x + o) % NX))
+        self.a = [n.copy(self.all(self.part, (n.x + o) % NX), self.all(self.got_x, o - 1), n.at(x=(n.x + o) % NX))
                   for o in range(1, NX)]
 
     def scatter_z(self):
@@ -73,31 +94,73 @@
                 total = total + self.got_x[o, k].astype(F32)
             self.row[k] = total.astype(BF16)
             return 0
-        lax.fori_loop(0, NZ, add, 0)
-        self.b = [n.copy(self.row.at[(n.z + o) % NZ], self.got_z.at[o - 1], n.at(z=(n.z + o) % NZ))
-                  for o in range(1, NZ)]
-
-    def gather_z(self):
-        n = self.net
+        lax.fori_loop(0, self.blocks, add, 0)
+        self.b = []
+        for o in range(1, NZ):
+            to = (n.z + o) % NZ
+            self.b.append(n.copy(self.row.at[self.block(to)], self.got_z.at[o - 1], n.at(z=to), self.keeps(to)))
+
+    def sum_z(self):
         for made in self.b:
             made.wait_recv()
-        total = self.row[n.z].astype(F32)
+        total = self.row[self.block(self.net.z)].astype(F32)
         for o in range(NZ - 1):
             total = total + self.got_z[o].astype(F32)
-        self.full[n.x, n.z] = total.astype(BF16)
-        self.d = [n.copy(self.full.at[n.x, n.z], self.full.at[n.x, n.z], n.at(z=(n.z + o) % NZ))
+        return total
+
+    def gather_z(self):
+        n = self.net
+        mine = self.block(n.z)
+
+        def settle():
+            self.full[n.x, mine] = self.sum_z().astype(BF16)
+        given(self.keeps(n.z), settle)
+        self.d = [n.copy(self.full.at[n.x, mine], self.full.at[n.x, mine], n.at(z=(n.z + o) % NZ), self.keeps(n.z))
                   for o in range(1, NZ)]
 
     def gather_x(self):
         n = self.net
-        for made in self.d:
-            made.wait_recv()
-        self.e = [n.copy(self.full.at[n.x], self.full.at[n.x], n.at(x=(n.x + o) % NX))
-                  for o in range(1, NX)]
+        for o, made in enumerate(self.d, 1):
+            given(self.keeps((n.z + NZ - o) % NZ), made.wait_recv)
+        own = self.all(self.full, n.x)
+        self.e = [n.copy(own, own, n.at(x=(n.x + o) % NX)) for o in range(1, NX)]
 
     def done(self):
         for made in self.e:
             made.wait_recv()
+
+
+class ScatterZX:
+    def __init__(self, net, part, got_z, row, got_x):
+        self.net, self.part, self.got_z, self.row, self.got_x = net, part, got_z, row, got_x
+
+    def scatter_z(self):
+        n = self.net
+        self.a = [n.copy(self.part.at[(n.z + o) % NZ], self.got_z.at[o - 1], n.at(z=(n.z + o) % NZ))
+                  for o in range(1, NZ)]
+
+    def scatter_x(self):
+        n = self.net
+        for made in self.a:
+            made.wait_recv()
+
+        def add(k, _):
+            total = self.part[n.z, k].astype(F32)
+            for o in range(NZ - 1):
+                total = total + self.got_z[o, k].astype(F32)
+            self.row[k] = total.astype(BF16)
+            return 0
+        lax.fori_loop(0, NX, add, 0)
+        self.b = [n.copy(self.row.at[(n.x + o) % NX], self.got_x.at[o - 1], n.at(x=(n.x + o) % NX))
+                  for o in range(1, NX)]
+
+    def sum_x(self):
+        for made in self.b:
+            made.wait_recv()
+        total = self.row[self.net.x].astype(F32)
+        for o in range(NX - 1):
+            total = total + self.got_x[o].astype(F32)
+        return total
 
 
 class GatherDp:
@@ -167,7 +230,7 @@
 
 def body(x_hbm, g_hbm, w_hbm, ei_hbm, di_hbm, eo_hbm, do_hbm, post_ref, gin_ref,
          xin, g, w, ei, di, eo, do, part, got_x, row, got_z, full, edits, grads, total, cot,
-         bpart, bgot_x, brow, bgot_z, send, recv, load):
+         bpart, bgot_x, brow, bgot_z, zpart, zgot_z, zrow, zgot_x, send, recv, load):
     net = Links(send, recv)
     z, x, y, c = net.z, net.x, net.y, net.c
     d = y * 2 + c
@@ -191,7 +254,8 @@
 
     def rows_of(ref):
         def pick(slot, half):
-            return ref.at[slot, pl.ds(0, TOK)] if half is None else ref.at[slot, pl.ds(half * (TOK // 2), TOK // 2)]
+            count = TOK if half is None else TOK // 2
+            return ref.at[pl.ds(pl.multiple_of(slot * TOK + (half or 0) * count, 32), count)]
         return pick
 
     whole_w = GatherDp(net, w_part)
@@ -216,7 +280,8 @@
         out[:, 7, :, 128:256] = fold.astype(BF16).reshape(NX, ROWS, 128)
 
     reduce_in, reduce_out, reduce_kernel, reduce_back = [
-        AllReduce(net, part.at[k], got_x.at[k], row.at[k], got_z.at[k], full.at[k]) for k in range(4)]
+        AllReduce(net, part.at[k], got_x.at[k], row.at[k], got_z.at[k], full.at[k], 8 if k < 2 else 6)
+        for k in range(4)]
 
     loads[1].wait()
     project(own, ei, part.at[0])
@@ -224,19 +289,17 @@
     loads[2].wait()
     loads[3].wait()
     project(g[...], eo, part.at[1])
-    reduce_out.scatter_x()
-    edits[:, pl.ds(TOK, 256 - TOK)] = jnp.zeros((8, 256 - TOK, 256), BF16)
-    grads[:, pl.ds(TOK, 256 - TOK)] = jnp.zeros((8, 256 - TOK, 512), BF16)
+    total[...] = jnp.zeros_like(total)
     for made in loads[4:]:
         made.wait()
     whole_in.step()
     reduce_in.scatter_z()
+    reduce_out.scatter_x()
+    reduce_in.gather_z()
+    reduce_in.gather_x()
+    whole_in.step()
     reduce_out.scatter_z()
-    reduce_in.gather_z()
     reduce_out.gather_z()
-    whole_in.step()
-    reduce_in.gather_x()
-    reduce_out.gather_x()
     whole_w.relay()
 
     def edit(value, hidden, dec, features):
@@ -253,31 +316,32 @@
     gather_edits = GatherDp(net, rows_of(edits))
     gather_grads = GatherDp(net, rows_of(grads))
     reduce_in.done()
-    edits[d, pl.ds(0, TOK)] = edit(own, full.at[0], di, D)
+    rows_own = pl.ds(pl.multiple_of(d * TOK, 64), TOK)
+    edits[rows_own, :] = edit(own, full.at[0], di, D)
     gather_edits.start()
-    reduce_out.done()
-    grads[d, pl.ds(0, TOK)] = edit(g[...], full.at[1], do, FW)
-    gather_grads.start()
+    reduce_out.gather_x()
     gather_edits.relay()
     gather_edits.relay_far()
     gather_edits.done()
 
     def inner(k, _):
-        part[2, :, k] = nt(own, edits[k]).astype(BF16).reshape(NX, ROWS, 256)
-        return 0
-    lax.fori_loop(0, 8, inner, 0)
+        part[2, :, k] = nt(own, edits[pl.ds(pl.multiple_of(k * 256, 256), 256), :]).astype(BF16).reshape(NX, ROWS, 256)
+        return 0
+    lax.fori_loop(0, 6, inner, 0)
     reduce_kernel.scatter_x()
+    whole_in.step()
+    reduce_out.done()
+    grads[rows_own, :] = edit(g[...], full.at[1], do, FW)
+    gather_grads.start()
+    reduce_kernel.scatter_z()
     gather_grads.relay()
+    whole_w.relay_far()
+    reduce_kernel.gather_z()
     whole_in.step()
-    whole_w.relay_far()
-    reduce_kernel.scatter_z()
     gather_grads.relay_far()
-    whole_in.step()
-    reduce_kernel.gather_z()
+    reduce_kernel.gather_x()
     whole_w.done()
     whole_in.step()
-
-    total[...] = jnp.zeros_like(total)
 
     def base(k, _):
         value = nn(xin[k, 0], w[k, 0])
@@ -286,15 +350,14 @@
         total[...] += value
         return 0
     lax.fori_loop(0, NZ, base, 0)
-    reduce_kernel.gather_x()
     gather_grads.done()
     reduce_kernel.done()
 
     def correct(k, _):
         block = (full[2, :, k].astype(F32) * FACTOR).astype(BF16).reshape(TOK, 256)
-        total[...] -= nn(block, grads[k])
-        return 0
-    lax.fori_loop(0, 8, correct, 0)
+        total[...] -= nn(block, grads[pl.ds(pl.multiple_of(k * 256, 256), 256), :])
+        return 0
+    lax.fori_loop(0, 6, correct, 0)
 
     def activate(k, _):
         rows = pl.ds(k * ROWS, ROWS)
@@ -306,50 +369,45 @@
     lax.fori_loop(0, NX, activate, 0)
 
     def back_inner(k, _):
-        part[3, :, k] = nt(cot[...], grads[k]).astype(BF16).reshape(NX, ROWS, 256)
-        return 0
-    lax.fori_loop(0, 8, back_inner, 0)
+        some = grads[pl.ds(pl.multiple_of(k * 256, 256), 256), :]
+        part[3, :, k] = nt(cot[...], some).astype(BF16).reshape(NX, ROWS, 256)
+        return 0
+    lax.fori_loop(0, 6, back_inner, 0)
     reduce_back.scatter_x()
 
-    def back_for(j):
-        def one(k, _):
-            bpart[j, k] = nt(cot[...], w[k, j]).astype(BF16)
-            return 0
-        lax.fori_loop(0, NZ, one, 0)
-
-    first = []
-    for o in range(1, NX):
-        j = (x + o) % NX
-        back_for(j)
-        first.append(net.copy(bpart.at[j], bgot_x.at[o - 1], net.at(x=j)))
-    back_for(x)
+    def back_block(k, _):
+        for j in range(NX):
+            value = nt(cot[...], w[k, j]).astype(BF16).reshape(NX, ROWS, 256)
+            for p in range(3):
+                bpart[p, j, k] = value[p]
+            zpart[k, j] = value[3]
+        return 0
+    lax.fori_loop(0, NZ, back_block, 0)
+    pieces = [AllReduce(net, bpart.at[p], bgot_x.at[p], brow.at[p], bgot_z.at[p], None) for p in range(3)]
+    last = ScatterZX(net, zpart, zgot_z, zrow, zgot_x)
+    last.scatter_z()
+    pieces[0].scatter_x()
     reduce_back.scatter_z()
+    pieces[1].scatter_x()
     reduce_back.gather_z()
+    pieces[2].scatter_x()
+    pieces[0].scatter_z()
     reduce_back.gather_x()
-    for made in first:
-        made.wait_recv()
-
-    def back_add(k, _):
-        value = bpart[x, k].astype(F32)
-        for o in range(NX - 1):
-            value = value + bgot_x[o, k].astype(F32)
-        brow[k] = value.astype(BF16)
-        return 0
-    lax.fori_loop(0, NZ, back_add, 0)
-    second = [net.copy(brow.at[(z + o) % NZ], bgot_z.at[o - 1], net.at(z=(z + o) % NZ)) for o in range(1, NZ)]
+    last.scatter_x()
+    pieces[1].scatter_z()
+    pieces[2].scatter_z()
     reduce_back.done()
     result = jnp.zeros((TOK, 256), F32)
-    for k in range(8):
+    for k in range(6):
         block = (full[3, :, k].astype(F32) * FACTOR).astype(BF16).reshape(TOK, 256)
-        result = result - nn(block, edits[k])
-    result = result + brow[z].astype(F32)
-    for o, made in enumerate(second):
-        made.wait_recv()
-        result = result + bgot_z[o].astype(F32)
-    gin_ref[...] = result.astype(BF16)
-
-    for made in net.sent:
-        made.wait_send()
+        result = result - nn(block, edits[256 * k:256 * k + 256, :])
+    sums = [last.sum_x()]
+    sums = [piece.sum_z() for piece in pieces] + sums
+    for p in range(NX):
+        rows = slice(ROWS * p, ROWS * p + ROWS)
+        gin_ref[rows, :] = (result[rows] + sums[p]).astype(BF16)
+
+    net.finish()
 
 
 COPIES = 160
@@ -371,14 +429,18 @@
         pltpu.VMEM((4, NZ, ROWS, 256), BF16),
         pltpu.VMEM((4, NZ - 1, ROWS, 256), BF16),
         pltpu.VMEM((4, NX, NZ, ROWS, 256), BF16),
-        pltpu.VMEM((8, 256, 256), BF16),
-        pltpu.VMEM((8, 256, 512), BF16),
+        pltpu.VMEM((8 * TOK, 256), BF16),
+        pltpu.VMEM((8 * TOK, 512), BF16),
         pltpu.VMEM((TOK, 512), F32),
         pltpu.VMEM((TOK, 512), BF16),
-        pltpu.VMEM((NX, NZ, TOK, 256), BF16),
-        pltpu.VMEM((NX - 1, NZ, TOK, 256), BF16),
-        pltpu.VMEM((NZ, TOK, 256), BF16),
-        pltpu.VMEM((NZ - 1, TOK, 256), BF16),
+        pltpu.VMEM((3, NX, NZ, ROWS, 256), BF16),
+        pltpu.VMEM((3, NX - 1, NZ, ROWS, 256), BF16),
+        pltpu.VMEM((3, NZ, ROWS, 256), BF16),
+        pltpu.VMEM((3, NZ - 1, ROWS, 256), BF16),
+        pltpu.VMEM((NZ, NX, ROWS, 256), BF16),
+        pltpu.VMEM((NZ - 1, NX, ROWS, 256), BF16),
+        pltpu.VMEM((NX, ROWS, 256), BF16),
+        pltpu.VMEM((NX - 1, ROWS, 256), BF16),
         pltpu.SemaphoreType.DMA((COPIES,)),
         pltpu.SemaphoreType.DMA((COPIES,)),
         pltpu.SemaphoreType.DMA((7,)),

time: 189 us -> 160 us (0.85); the launches traced: 186 us -> 159 us
  Pallas kernels: 182 us -> 156 us
    pallas_call x1, Pallas kernels: 182 us -> 156 us  [shards(): pl.pallas_call(body, out_shape=(jax.ShapeDtypeStruct((TOK, 512), BF16), j...]
where the time goes in v2:
time: 160 us; the launch traced here: 159 us
  Pallas kernels  156 us (98%)
  local copies, waits for them, and re-layouts  3.16 us (2%)
    pallas_call x1, Pallas kernels, shards(): pl.pallas_call(body, out_shape=(jax.ShapeDtypeStruct((TOK, 512), BF16), j...  156 us

profile of v2, /device:TPU:8, one launch (start us, length us, event | category | flops | bytes accessed | tf_op | source)
XLA Modules:
  0.0 159.4 jit_solution(11593551952302153012)
XLA Ops:
  0.6 155.6 %shard_map.86 = (bf16[192,512]{1,0:T(8,128)(2,1)}, bf16[192,256]{1,0:T(8,128)(2,1)}) custom-call(bf16[192,256]{1,0:T(8,128)(2,1)} %x_hbm.1, bf16[192,512]{1,0:T(8,128)(2,1)} %g_hbm.1, bf16[4,256,512]{2,1,0:T(8,128)(2,1)} %bitcast.1, bf16[256,1920]{1,0:T(8,128)(2,1)} %ei_hbm.1, bf16[1920,256]{1,0:T(8,128)(2,1)} %di_hbm.1, bf16[512,1920]{1,0:T(8,128)(2,1)} %eo_hbm.1, ...), custom_call_target="tpu_custom_call" | custom-call | tf_op jit(solution)/shard_map/pallas_call | solution.py:448
  156.2 1.6 %copy.11 = bf16[192,512]{1,0:T(8,128)(2,1)} copy(bf16[192,512]{1,0:T(8,128)(2,1)} %get-tuple-element.4) | data formatting | bytes 393216
  157.8 1.5 copy.12

commit v3 on v2

--- a/solution.py
+++ b/solution.py
@@ -194,6 +194,28 @@
         self.over.append(n.copy(self.part(far, 0), self.part(far, 0), n.at(c=1 - n.c)))
         self.down2.wait_recv()
         self.over.append(n.copy(self.part(far, 1), self.part(far, 1), n.at(c=1 - n.c)))
+
+    def done(self):
+        for made in self.over:
+            made.wait_recv()
+
+
+class GatherNear:
+    def __init__(self, net, part):
+        self.net, self.part = net, part
+
+    def start(self):
+        n = self.net
+        own = self.part(n.y * 2 + n.c, None)
+        self.near = [n.copy(own, own, n.at(y=(n.y + o) % NY)) for o in (1, 3, 2)]
+        self.over = [n.copy(own, own, n.at(c=1 - n.c))]
+
+    def relay(self):
+        n = self.net
+        for o, made in zip((1, 3, 2), self.near):
+            made.wait_recv()
+            slot = self.part((n.y + NY - o) % NY * 2 + n.c, None)
+            self.over.append(n.copy(slot, slot, n.at(c=1 - n.c)))
 
     def done(self):
         for made in self.over:
@@ -244,10 +266,9 @@
 
     barrier = pltpu.get_barrier_semaphore()
     peers = ([net.at(x=(x + o) % NX) for o in range(1, NX)] + [net.at(z=(z + o) % NZ) for o in range(1, NZ)]
-             + [net.at(y=(y + 1) % NY), net.at(y=(y + NY - 1) % NY), net.at(c=1 - c)])
+             + [net.at(y=(y + o) % NY) for o in range(1, NY)] + [net.at(c=1 - c)])
     for peer in peers:
         pl.semaphore_signal(barrier, inc=1, device_id=peer, device_id_type=MESH)
-    pl.semaphore_wait(barrier, len(peers))
 
     def w_part(slot, half):
         return w.at[slot] if half is None else w.at[slot, pl.ds(2 * half, 2)]
@@ -259,11 +280,8 @@
         return pick
 
     whole_w = GatherDp(net, w_part)
-    whole_w.start(w_hbm)
+    whole_in = GatherMp(net, xin)
     loads[0].wait()
-    whole_in = GatherMp(net, xin)
-    whole_in.start()
-
     own = xin[z, x]
 
     def project(value, enc, out):
@@ -285,22 +303,22 @@
 
     loads[1].wait()
     project(own, ei, part.at[0])
+    pl.semaphore_wait(barrier, len(peers))
     reduce_in.scatter_x()
+    whole_w.start(w_hbm)
     loads[2].wait()
     loads[3].wait()
     project(g[...], eo, part.at[1])
     total[...] = jnp.zeros_like(total)
     for made in loads[4:]:
         made.wait()
-    whole_in.step()
     reduce_in.scatter_z()
     reduce_out.scatter_x()
+    whole_in.start()
     reduce_in.gather_z()
     reduce_in.gather_x()
     whole_in.step()
     reduce_out.scatter_z()
-    reduce_out.gather_z()
-    whole_w.relay()
 
     def edit(value, hidden, dec, features):
         squares = hidden[:, 7, :, 128:256].astype(F32).reshape(TOK, 128)
@@ -313,35 +331,37 @@
             out = out + nn(h, dec[256 * k:256 * k + width, :])
         return out.astype(BF16)
 
-    gather_edits = GatherDp(net, rows_of(edits))
-    gather_grads = GatherDp(net, rows_of(grads))
+    gather_edits = GatherNear(net, rows_of(edits))
+    gather_grads = GatherNear(net, rows_of(grads))
     reduce_in.done()
     rows_own = pl.ds(pl.multiple_of(d * TOK, 64), TOK)
     edits[rows_own, :] = edit(own, full.at[0], di, D)
     gather_edits.start()
-    reduce_out.gather_x()
+    reduce_out.gather_z()
     gather_edits.relay()
-    gather_edits.relay_far()
     gather_edits.done()
 
     def inner(k, _):
-        part[2, :, k] = nt(own, edits[pl.ds(pl.multiple_of(k * 256, 256), 256), :]).astype(BF16).reshape(NX, ROWS, 256)
+        some = edits[pl.ds(pl.multiple_of(k * 256, 256), 256), :]
+        part[2, :, k] = nt(own, some).astype(BF16).reshape(NX, ROWS, 256)
         return 0
     lax.fori_loop(0, 6, inner, 0)
     reduce_kernel.scatter_x()
+    whole_in.step()
+    reduce_out.gather_x()
+    whole_w.relay()
+    reduce_kernel.scatter_z()
     whole_in.step()
     reduce_out.done()
     grads[rows_own, :] = edit(g[...], full.at[1], do, FW)
     gather_grads.start()
-    reduce_kernel.scatter_z()
-    gather_grads.relay()
-    whole_w.relay_far()
     reduce_kernel.gather_z()
     whole_in.step()
-    gather_grads.relay_far()
+    whole_w.relay_far()
+    gather_grads.relay()
     reduce_kernel.gather_x()
+    whole_in.step()
     whole_w.done()
-    whole_in.step()
 
     def base(k, _):
         value = nn(xin[k, 0], w[k, 0])
@@ -410,7 +430,7 @@
     net.finish()
 
 
-COPIES = 160
+COPIES = 176
 
 
 def shards(inputs, out_grads, weight, enc_in, dec_in, enc_out, dec_out):

time: 160 us -> 150 us (0.938)
  Pallas kernels: 156 us -> 145 us
    pallas_call x1, Pallas kernels: 156 us -> 145 us  [shards(): pl.pallas_call(body, out_shape=(jax.ShapeDtypeStruct((TOK, 512), BF16), j...]
where the time goes in v3:
time: 150 us; the launch traced here: 148 us
  Pallas kernels  145 us (97%)
  local copies, waits for them, and re-layouts  3.16 us (2%)
    pallas_call x1, Pallas kernels, shards(): pl.pallas_call(body, out_shape=(jax.ShapeDtypeStruct((TOK, 512), BF16), j...  145 us
    unnamed x2, local copies, waits for them, and re-layouts  3.16 us

profile of v3, /device:TPU:8, one launch (start us, length us, event | category | flops | bytes accessed | tf_op | source)
XLA Modules:
  0.0 148.4 jit_solution(16306556575489195901)
XLA Ops:
  0.6 144.6 %shard_map.86 = (bf16[192,512]{1,0:T(8,128)(2,1)}, bf16[192,256]{1,0:T(8,128)(2,1)}) custom-call(bf16[192,256]{1,0:T(8,128)(2,1)} %x_hbm.1, bf16[192,512]{1,0:T(8,128)(2,1)} %g_hbm.1, bf16[4,256,512]{2,1,0:T(8,128)(2,1)} %bitcast.1, bf16[256,1920]{1,0:T(8,128)(2,1)} %ei_hbm.1, bf16[1920,256]{1,0:T(8,128)(2,1)} %di_hbm.1, bf16[512,1920]{1,0:T(8,128)(2,1)} %eo_hbm.1, ...), custom_call_target="tpu_custom_call" | custom-call | tf_op jit(solution)/shard_map/pallas_call | solution.py:468
  145.2 1.6 %copy.11 = bf16[192,512]{1,0:T(8,128)(2,1)} copy(bf16[192,512]{1,0:T(8,128)(2,1)} %get-tuple-element.4) | data formatting | bytes 393216
  146.9 1.5 %copy.12 = bf16[192,256]{1,0:T(8,128)(2,1)} copy(bf16[192,256]{1,0:T(8,128)(2,1)} %get-tuple-element.5) | data formatting | bytes 196608

commit v4 on v3

--- a/solution.py
+++ b/solution.py
@@ -339,6 +339,7 @@
     gather_edits.start()
     reduce_out.gather_z()
     gather_edits.relay()
+    whole_in.step()
     gather_edits.done()
 
     def inner(k, _):
@@ -347,19 +348,18 @@
         return 0
     lax.fori_loop(0, 6, inner, 0)
     reduce_kernel.scatter_x()
-    whole_in.step()
-    reduce_out.gather_x()
     whole_w.relay()
     reduce_kernel.scatter_z()
+    reduce_out.gather_x()
     whole_in.step()
+    reduce_kernel.gather_z()
     reduce_out.done()
     grads[rows_own, :] = edit(g[...], full.at[1], do, FW)
     gather_grads.start()
-    reduce_kernel.gather_z()
     whole_in.step()
     whole_w.relay_far()
+    reduce_kernel.gather_x()
     gather_grads.relay()
-    reduce_kernel.gather_x()
     whole_in.step()
     whole_w.done()
 
@@ -405,17 +405,17 @@
     lax.fori_loop(0, NZ, back_block, 0)
     pieces = [AllReduce(net, bpart.at[p], bgot_x.at[p], brow.at[p], bgot_z.at[p], None) for p in range(3)]
     last = ScatterZX(net, zpart, zgot_z, zrow, zgot_x)
+    pieces[0].scatter_x()
     last.scatter_z()
-    pieces[0].scatter_x()
     reduce_back.scatter_z()
     pieces[1].scatter_x()
-    reduce_back.gather_z()
     pieces[2].scatter_x()
     pieces[0].scatter_z()
+    reduce_back.gather_z()
+    pieces[1].scatter_z()
+    last.scatter_x()
+    pieces[2].scatter_z()
     reduce_back.gather_x()
-    last.scatter_x()
-    pieces[1].scatter_z()
-    pieces[2].scatter_z()
     reduce_back.done()
     result = jnp.zeros((TOK, 256), F32)
     for k in range(6):

time: 150 us -> 148 us (0.987)
  Pallas kernels: 145 us -> 142 us
    pallas_call x1, Pallas kernels: 145 us -> 142 us  [shards(): pl.pallas_call(body, out_shape=(jax.ShapeDtypeStruct((TOK, 512), BF16), j...]
where the time goes in v4:
time: 148 us; the launch traced here: 146 us
  Pallas kernels  142 us (96%)
  local copies, waits for them, and re-layouts  3.16 us (2%)
    pallas_call x1, Pallas kernels, shards(): pl.pallas_call(body, out_shape=(jax.ShapeDtypeStruct((TOK, 512), BF16), j...  142 us
    unnamed x2, local copies, waits for them, and re-layouts  3.16 us

profile of v4, /device:TPU:8, one launch (start us, length us, event | category | flops | bytes accessed | tf_op | source)
XLA Modules:
  0.0 145.6 jit_solution(9075750943841119846)
XLA Ops:
  0.6 141.8 %shard_map.86 = (bf16[192,512]{1,0:T(8,128)(2,1)}, bf16[192,256]{1,0:T(8,128)(2,1)}) custom-call(bf16[192,256]{1,0:T(8,128)(2,1)} %x_hbm.1, bf16[192,512]{1,0:T(8,128)(2,1)} %g_hbm.1, bf16[4,256,512]{2,1,0:T(8,128)(2,1)} %bitcast.1, bf16[256,1920]{1,0:T(8,128)(2,1)} %ei_hbm.1, bf16[1920,256]{1,0:T(8,128)(2,1)} %di_hbm.1, bf16[512,1920]{1,0:T(8,128)(2,1)} %eo_hbm.1, ...), custom_call_target="tpu_custom_call" | custom-call | tf_op jit(solution)/shard_map/pallas_call | solution.py:468
  142.4 1.6 %copy.11 = bf16[192,512]{1,0:T(8,128)(2,1)} copy(bf16[192,512]{1,0:T(8,128)(2,1)} %get-tuple-element.4) | data formatting | bytes 393216
  144.0 1.5 %copy.12 = bf16[192,256]{1,0:T(8,128)(2,1)} copy(bf16[192,256]{1,0:T(8,128)(2,1)} %get-tuple-element.5) | data formatting | bytes 196608

commit v5 on v4

--- a/solution.py
+++ b/solution.py
@@ -239,13 +239,15 @@
                 made.wait_recv()
         else:
             self.up.wait_recv()
-            if s <= NZ // 2 - 1:
-                self.down.wait_recv()
+            self.down.wait_recv()
         if s < NZ // 2:
-            up = self.block.at[(n.z + NZ - s) % NZ]
+            up, down = (n.z + NZ - s) % NZ, (n.z + s) % NZ
+            if s < NZ // 2 - 1:
+                up, down = self.block.at[up], self.block.at[down]
+            else:
+                half = NX // 2
+                up, down = self.block.at[up, pl.ds(0, half)], self.block.at[down, pl.ds(half, half)]
             self.up = n.copy(up, up, n.at(z=(n.z + 1) % NZ))
-        if s < NZ // 2 - 1:
-            down = self.block.at[(n.z + s) % NZ]
             self.down = n.copy(down, down, n.at(z=(n.z + NZ - 1) % NZ))
         self.s += 1
 

time: 148 us -> 145 us (0.980); the launches traced: 146 us -> 144 us
  Pallas kernels: 142 us -> 140 us
where the time goes in v5:
time: 145 us; the launch traced here: 144 us
  Pallas kernels  140 us (97%)
  local copies, waits for them, and re-layouts  3.16 us (2%)
    pallas_call x1, Pallas kernels, shards(): pl.pallas_call(body, out_shape=(jax.ShapeDtypeStruct((TOK, 512), BF16), j...  140 us
    unnamed x2, local copies, waits for them, and re-layouts  3.16 us

profile of v5, /device:TPU:8, one launch (start us, length us, event | category | flops | bytes accessed | tf_op | source)
XLA Modules:
  0.0 144.1 jit_solution(16767893276901693765)
XLA Ops:
  0.6 140.3 %shard_map.86 = (bf16[192,512]{1,0:T(8,128)(2,1)}, bf16[192,256]{1,0:T(8,128)(2,1)}) custom-call(bf16[192,256]{1,0:T(8,128)(2,1)} %x_hbm.1, bf16[192,512]{1,0:T(8,128)(2,1)} %g_hbm.1, bf16[4,256,512]{2,1,0:T(8,128)(2,1)} %bitcast.1, bf16[256,1920]{1,0:T(8,128)(2,1)} %ei_hbm.1, bf16[1920,256]{1,0:T(8,128)(2,1)} %di_hbm.1, bf16[512,1920]{1,0:T(8,128)(2,1)} %eo_hbm.1, ...), custom_call_target="tpu_custom_call" | custom-call | tf_op jit(solution)/shard_map/pallas_call | solution.py:470
  141.0 1.6 %copy.11 = bf16[192,512]{1,0:T(8,128)(2,1)} copy(bf16[192,512]{1,0:T(8,128)(2,1)} %get-tuple-element.4) | data formatting | bytes 393216
  142.6 1.5 %copy.12 = bf16[192,256]{1,0:T(8,128)(2,1)} copy(bf16[192,256]{1,0:T(8,128)(2,1)} %get-tuple-element.5) | data formatting | bytes 196608

commit v6 on v5

--- a/solution.py
+++ b/solution.py
@@ -355,10 +355,10 @@
     reduce_out.gather_x()
     whole_in.step()
     reduce_kernel.gather_z()
+    whole_in.step()
     reduce_out.done()
     grads[rows_own, :] = edit(g[...], full.at[1], do, FW)
     gather_grads.start()
-    whole_in.step()
     whole_w.relay_far()
     reduce_kernel.gather_x()
     gather_grads.relay()

time: 145 us -> 148 us (1.021)
  Pallas kernels: 140 us -> 144 us
    pallas_call x1, Pallas kernels: 140 us -> 144 us  [shards(): pl.pallas_call(body, out_shape=(jax.ShapeDtypeStruct((TOK, 512), BF16), j...]
where the time goes in v6:
time: 148 us
  Pallas kernels  144 us (97%)
  local copies, waits for them, and re-layouts  3.16 us (2%)
    pallas_call x1, Pallas kernels, shards(): pl.pallas_call(body, out_shape=(jax.ShapeDtypeStruct((TOK, 512), BF16), j...  144 us
    unnamed x2, local copies, waits for them, and re-layouts  3.16 us

profile of v6, /device:TPU:8, one launch (start us, length us, event | category | flops | bytes accessed | tf_op | source)
XLA Modules:
  0.0 147.5 jit_solution(420985436841475950)
XLA Ops:
  0.6 143.7 %shard_map.86 = (bf16[192,512]{1,0:T(8,128)(2,1)}, bf16[192,256]{1,0:T(8,128)(2,1)}) custom-call(bf16[192,256]{1,0:T(8,128)(2,1)} %x_hbm.1, bf16[192,512]{1,0:T(8,128)(2,1)} %g_hbm.1, bf16[4,256,512]{2,1,0:T(8,128)(2,1)} %bitcast.1, bf16[256,1920]{1,0:T(8,128)(2,1)} %ei_hbm.1, bf16[1920,256]{1,0:T(8,128)(2,1)} %di_hbm.1, bf16[512,1920]{1,0:T(8,128)(2,1)} %eo_hbm.1, ...), custom_call_target="tpu_custom_call" | custom-call | tf_op jit(solution)/shard_map/pallas_call | solution.py:470
  144.3 1.6 %copy.11 = bf16[192,512]{1,0:T(8,128)(2,1)} copy(bf16[192,512]{1,0:T(8,128)(2,1)} %get-tuple-element.4) | data formatting | bytes 393216
  146.0 1.5 %copy.12 = bf16[192,256]{1,0:T(8,128)(2,1)} copy(bf16[192,256]{1,0:T(8,128)(2,1)} %get-tuple-element.5) | data formatting | bytes 196608

commit v7 on v5

--- a/solution.py
+++ b/solution.py
@@ -65,6 +65,8 @@
 
 
 class AllReduce:
+    arrivals = NX - 1
+
     def __init__(self, net, part, got_x, row, got_z, full, blocks=NZ):
         self.net, self.part, self.got_x, self.row, self.got_z, self.full = net, part, got_x, row, got_z, full
         self.blocks = blocks
@@ -90,7 +92,7 @@
 
         def add(k, _):
             total = self.part[n.x, k].astype(F32)
-            for o in range(NX - 1):
+            for o in range(self.arrivals):
                 total = total + self.got_x[o, k].astype(F32)
             self.row[k] = total.astype(BF16)
             return 0
@@ -128,6 +130,32 @@
     def done(self):
         for made in self.e:
             made.wait_recv()
+
+
+class RelayedScatter(AllReduce):
+    arrivals = 2
+
+    def scatter_x(self):
+        n, half = self.net, NZ // 2
+        far = (n.x + 2) % NX
+        low, high = pl.ds(0, half), pl.ds(half, half)
+        self.far_up = n.copy(self.part.at[far, low], self.got_x.at[2, low], n.at(x=(n.x + 1) % NX))
+        self.far_down = n.copy(self.part.at[far, high], self.got_x.at[2, high], n.at(x=(n.x + 3) % NX))
+
+    def relay_x(self):
+        n, half = self.net, NZ // 2
+        up, down = (n.x + 1) % NX, (n.x + 3) % NX
+        self.far_up.wait_recv()
+        self.far_down.wait_recv()
+
+        def add(k, _):
+            self.part[up, k] = (self.part[up, k].astype(F32) + self.got_x[2, k].astype(F32)).astype(BF16)
+            h = k + half
+            self.part[down, h] = (self.part[down, h].astype(F32) + self.got_x[2, h].astype(F32)).astype(BF16)
+            return 0
+        lax.fori_loop(0, half, add, 0)
+        self.a = [n.copy(self.part.at[up], self.got_x.at[0], n.at(x=up)),
+                  n.copy(self.part.at[down], self.got_x.at[1], n.at(x=down))]
 
 
 class ScatterZX:
@@ -405,14 +433,17 @@
             zpart[k, j] = value[3]
         return 0
     lax.fori_loop(0, NZ, back_block, 0)
-    pieces = [AllReduce(net, bpart.at[p], bgot_x.at[p], brow.at[p], bgot_z.at[p], None) for p in range(3)]
+    pieces = [RelayedScatter(net, bpart.at[p], bgot_x.at[p], brow.at[p], bgot_z.at[p], None) for p in range(3)]
     last = ScatterZX(net, zpart, zgot_z, zrow, zgot_x)
     pieces[0].scatter_x()
     last.scatter_z()
+    pieces[1].scatter_x()
     reduce_back.scatter_z()
-    pieces[1].scatter_x()
+    pieces[0].relay_x()
     pieces[2].scatter_x()
+    pieces[1].relay_x()
     pieces[0].scatter_z()
+    pieces[2].relay_x()
     reduce_back.gather_z()
     pieces[1].scatter_z()
     last.scatter_x()

time: 145 us -> 145 us (level)
  no operation moved by 1% of the time
where the time goes in v7:
time: 145 us; the launch traced here: 144 us
  Pallas kernels  140 us (97%)
  local copies, waits for them, and re-layouts  3.16 us (2%)
    pallas_call x1, Pallas kernels, shards(): pl.pallas_call(body, out_shape=(jax.ShapeDtypeStruct((TOK, 512), BF16), j...  140 us
    unnamed x2, local copies, waits for them, and re-layouts  3.16 us

profile of v7, /device:TPU:8, one launch (start us, length us, event | category | flops | bytes accessed | tf_op | source)
XLA Modules:
  0.0 143.6 jit_solution(11016042407962059314)
XLA Ops:
  0.6 139.8 %shard_map.86 = (bf16[192,512]{1,0:T(8,128)(2,1)}, bf16[192,256]{1,0:T(8,128)(2,1)}) custom-call(bf16[192,256]{1,0:T(8,128)(2,1)} %x_hbm.1, bf16[192,512]{1,0:T(8,128)(2,1)} %g_hbm.1, bf16[4,256,512]{2,1,0:T(8,128)(2,1)} %bitcast.1, bf16[256,1920]{1,0:T(8,128)(2,1)} %ei_hbm.1, bf16[1920,256]{1,0:T(8,128)(2,1)} %di_hbm.1, bf16[512,1920]{1,0:T(8,128)(2,1)} %eo_hbm.1, ...), custom_call_target="tpu_custom_call" | custom-call | tf_op jit(solution)/shard_map/pallas_call | solution.py:501
  140.5 1.6 %copy.11 = bf16[192,512]{1,0:T(8,128)(2,1)} copy(bf16[192,512]{1,0:T(8,128)(2,1)} %get-tuple-element.4) | data formatting | bytes 393216
  142.1 1.5 %copy.12 = bf16[192,256]{1,0:T(8,128)(2,1)} copy(bf16[192,256]{1,0:T(8,128)(2,1)} %get-tuple-element.5) | data formatting | bytes 196608

commit v8 on v7

--- a/solution.py
+++ b/solution.py
@@ -446,9 +446,9 @@
     pieces[2].relay_x()
     reduce_back.gather_z()
     pieces[1].scatter_z()
+    reduce_back.gather_x()
+    pieces[2].scatter_z()
     last.scatter_x()
-    pieces[2].scatter_z()
-    reduce_back.gather_x()
     reduce_back.done()
     result = jnp.zeros((TOK, 256), F32)
     for k in range(6):

time: 145 us -> 145 us (level)
  no operation moved by 1% of the time
where the time goes in v8:
time: 145 us
  Pallas kernels  141 us (97%)
  local copies, waits for them, and re-layouts  3.16 us (2%)
    pallas_call x1, Pallas kernels, shards(): pl.pallas_call(body, out_shape=(jax.ShapeDtypeStruct((TOK, 512), BF16), j...  141 us
    unnamed x2, local copies, waits for them, and re-layouts  3.16 us

profile of v8, /device:TPU:8, one launch (start us, length us, event | category | flops | bytes accessed | tf_op | source)
XLA Modules:
  0.0 144.8 jit_solution(4502522103252510511)
XLA Ops:
  0.6 141.0 %shard_map.86 = (bf16[192,512]{1,0:T(8,128)(2,1)}, bf16[192,256]{1,0:T(8,128)(2,1)}) custom-call(bf16[192,256]{1,0:T(8,128)(2,1)} %x_hbm.1, bf16[192,512]{1,0:T(8,128)(2,1)} %g_hbm.1, bf16[4,256,512]{2,1,0:T(8,128)(2,1)} %bitcast.1, bf16[256,1920]{1,0:T(8,128)(2,1)} %ei_hbm.1, bf16[1920,256]{1,0:T(8,128)(2,1)} %di_hbm.1, bf16[512,1920]{1,0:T(8,128)(2,1)} %eo_hbm.1, ...), custom_call_target="tpu_custom_call" | custom-call | tf_op jit(solution)/shard_map/pallas_call | solution.py:501
  141.6 1.6 %copy.11 = bf16[192,512]{1,0:T(8,128)(2,1)} copy(bf16[192,512]{1,0:T(8,128)(2,1)} %get-tuple-element.4) | data formatting | bytes 393216
  143.3 1.5 %copy.12 = bf16[192,256]{1,0:T(8,128)(2,1)} copy(bf16[192,256]{1,0:T(8,128)(2,1)} %get-tuple-element.5) | data formatting | bytes 196608
